TPU v7x, 512 devices: a whole 4x4x16 slice. The times are simulated.
512 devices in a mesh: row: 16 (over x, y), col: 32 (over z, core).
Axes of the slice: x: 4, y: 4, z: 16, core: 2. Of those that a mesh axis runs over, the one named last changes fastest.
Arguments:
- trailing: float32 [4096, 4096], P('row', 'col'), may hold values from -6 to 6
- panel_block: float32 [4096, 1024], P('row', 'col'), may hold values from -1.2 to 1.2
- inverse: float32 [1024, 1024], P(None, 'col'), may hold values from -1 to 1.5, as said below
- checksum: float32 [4096, 128], P('row', 'col'), may hold values from -24 to 24
Outputs:
- updated: float32 [4096, 4096], P('row', 'col')
- checksum_new: float32 [4096, 128], P('row', 'col')
- reencoded: float32 [4096, 128], P('row', 'col')
Inputs may be any that keep to these rules, and one draw needn't show every extreme that they name: `inverse`: zero above the diagonal; the diagonal lies between 0.5 and 1.5.
All inputs are finite; a program needn't handle non-finite values.
Results may differ from a plain program's by a relative error of at most 0.00007.
Values sent between devices are 32-bit elements; how exact they have to be, the bound alone decides.
A program may use at most 64 MiB of HBM per device.

v0:
```python
import jax
import jax.numpy as jnp
from jax import lax
from jax.sharding import PartitionSpec as P


def spread(x, axis, root):
    mine = lax.axis_index(axis) == root
    return lax.psum(jnp.where(mine, x, jnp.zeros_like(x)), axis)


def times_transpose(first_matrix, second_matrix):
    return lax.dot_general(
        first_matrix,
        second_matrix,
        (((1,), (1,)), ((), ())),
        precision=lax.Precision.HIGHEST,
        preferred_element_type=jnp.float32,
    )


def on_device(trailing, panel_block, inverse, checksum):
    column_count = lax.axis_size("col")
    row_count = lax.axis_size("row")
    column_index = lax.axis_index("col")
    column_block = trailing.shape[1]
    quotient = column_count // row_count
    inverse_full = lax.all_gather(inverse, "col", axis=1, tiled=True)
    panel_rows = lax.all_gather(panel_block, "col", axis=1, tiled=True)
    factor_rows = times_transpose(panel_rows, inverse_full)
    piece_index = column_index % quotient
    owner_row = column_index // quotient
    owned_block = lax.dynamic_slice_in_dim(factor_rows, piece_index * column_block, column_block, 0)
    column_factor = spread(owned_block, "row", owner_row)
    updated = trailing - times_transpose(factor_rows, column_factor)
    slice_sum = lax.psum_scatter(column_factor, "col", scatter_dimension=0, tiled=True)
    correction = times_transpose(factor_rows, slice_sum)
    checksum_new = checksum - correction
    reencoded = lax.psum_scatter(updated, "col", scatter_dimension=1, tiled=True)
    return (updated, checksum_new, reencoded)


def solution(mesh):
    in_specs = (P("row", "col"), P("row", "col"), P(None, "col"), P("row", "col"))
    out_specs = (P("row", "col"), P("row", "col"), P("row", "col"))
    return jax.shard_map(
        on_device, mesh=mesh, in_specs=in_specs, out_specs=out_specs, check_vma=False
    )
```

profile of v0, /device:TPU:1, one launch (start us, length us, event | category | flops | bytes accessed | tf_op | source)
XLA Modules:
  0.0 497.4 jit_solution(3046070347477778227)
XLA Ops:
  7.2 0.0 copy-start
  7.2 0.0 all-gather.3.cloned.1.call-start
  7.2 0.7 all-gather.3.cloned.1.call-update
  7.9 0.0 all-gather.5.cloned.1.call-start
  8.0 0.7 all-gather.5.cloned.1.call-update
  8.7 0.0 all-reduce.6.cloned.1.call-start
  8.7 0.0 copy-start.1
  8.7 77.8 %all-gather.3.cloned.1.call-done = f32[256,1024]{0,1:T(8,128)} async-done(((f32[256,32]{0,1:T(8,128)}), f32[256,1024]{0,1:T(8,128)}) %all-gather.3.cloned.1.call-update) | async-done | bytes 1048592 | tf_op jit(solution)/shard_map/all_gather | solution.py:29
  86.5 73.1 %all-gather.5.cloned.1.call-done = f32[1024,1024]{0,1:T(8,128)} async-done(((f32[1024,32]{0,1:T(8,128)}), f32[1024,1024]{0,1:T(8,128)}) %all-gather.5.cloned.1.call-update) | async-done | bytes 4194320 | tf_op jit(solution)/shard_map/all_gather | solution.py:28
  159.6 5.8 %fusion.2 = f32[256,1024]{1,0:T(8,128)S(1)} fusion(f32[256,1024]{0,1:T(8,128)} %all-gather.3.cloned.1.call-done, f32[1024,1024]{0,1:T(8,128)} %all-gather.5.cloned.1.call-done), kind=kOutput, calls=%fused_computation.6 | convolution fusion | flops 3221225472 | bytes 6291456 | tf_op jit(solution)/shard_map/dot_general | solution.py:13
  165.4 0.8 dynamic-slice_select_fusion
  166.3 0.0 all-reduce.6.cloned.1.call-update
  166.3 0.0 all-reduce.8.cloned.1.call-start
  166.3 111.4 %all-reduce.6.cloned.1.call-done = f32[128,1024]{1,0:T(8,128)} async-done(((f32[128,1024]{1,0:T(8,128)}), f32[128,1024]{1,0:T(8,128)}) %all-reduce.6.cloned.1.call-update) | async-done | bytes 524304 | tf_op jit(solution)/shard_map/psum | solution.py:9
  277.8 0.0 copy-done
  277.8 2.7 convolution_subtract_fusion
  280.4 0.0 all-reduce.8.cloned.1.call-update
  280.5 1.3 dynamic-slice
  282.4 204.5 %all-reduce.8.cloned.1.call-done = (f32[128,1024]{1,0:T(8,128)}, f32[256,128]{1,0:T(8,128)}) async-done(((f32[128,1024]{1,0:T(8,128)}, f32[256,128]{1,0:T(8,128)}), (f32[128,1024]{1,0:T(8,128)}, f32[256,128]{1,0:T(8,128)})) %all-reduce.8.cloned.1.call-update) | async-done | bytes 655376
  486.9 1.0 constant_dynamic-slice_fusion
  487.9 0.7 copy.8
  488.6 0.0 copy-done.1
  488.6 2.3 convolution_subtract_fusion.1
Async XLA Ops:
  7.2 270.6 %copy-start = (f32[256,128]{1,0:T(8,128)S(1)}, f32[256,128]{1,0:T(8,128)}, u32[]{:S(2)}) copy-start(f32[256,128]{1,0:T(8,128)} %param.4) | copy-start | bytes 393220
  7.2 79.4 %all-gather.3.cloned.1.call-start = ((), (), s32[]{:S(2)}) async-start(), calls=%async_computation | async-start | bytes 1081344 | tf_op jit(solution)/shard_map/all_gather | solution.py:29
  7.9 151.7 %all-gather.5.cloned.1.call-start = ((), (), s32[]{:S(2)}) async-start(), calls=%async_computation.1 | async-start | bytes 4325376 | tf_op jit(solution)/shard_map/all_gather | solution.py:28
  8.7 269.1 %all-reduce.6.cloned.1.call-start = ((), (), s32[]{:S(2)}) async-start(), calls=%async_computation.2 | async-start | bytes 1048576 | tf_op jit(solution)/shard_map/psum | solution.py:9
  8.7 479.8 %copy-start.1 = (f32[256,4]{0,1:T(4,128)S(1)}, f32[256,4]{0,1:T(4,128)}, u32[]{:S(2)}) copy-start(f32[256,4]{0,1:T(4,128)} %param.7) | copy-start | bytes 12292
  166.3 320.6 %all-reduce.8.cloned.1.call-start = ((), (), s32[]{:S(2)}) async-start(), calls=%async_computation.3 | async-start | bytes 1310720
Sparse Core Ops, SparseCore 0:
  10.1 76.3 all-gather.2
  88.6 70.9 all-gather.4
  166.4 111.2 all-reduce.5
  280.7 206.1 all-reduce.7
where the time goes:
time: 498 us; the launch traced here: 497 us
  waiting for transfers between devices  468 us (94%)
  between operations  14.5 us (3%)
  matrix products  10.8 us (2%)
    unnamed x5, waiting for transfers between devices  206 us
    psum x1, waiting for transfers between devices, spread(): return lax.psum(jnp.where(mine, x, jnp.zeros_like(x)), axis)  111 us
    all_gather x1, waiting for transfers between devices, on_device(): panel_rows = lax.all_gather(panel_block, 'col', axis=1, tiled=True)  77.8 us
    all_gather x1, waiting for transfers between devices, on_device(): inverse_full = lax.all_gather(inverse, 'col', axis=1, tiled=True)  73.1 us
    dot_general x3, matrix products, times_transpose(): lax.dot_general(first_matrix, second_matrix, (((1,), (1,)), ((), ())), pr...  10.8 us
  transfers between devices with their start and end apart: 4, of which 4 were waited for; matrix products, arithmetic and copies ran while one was open for 0% of the time, Pallas kernels for 0%

commit v1 on v0

v1 whole, which is shorter than its diff:
```python
import jax
import jax.numpy as jnp
from jax import lax
from jax.experimental import pallas as pl
from jax.experimental.pallas import tpu as pltpu
from jax.sharding import PartitionSpec as P

F32, BF16 = jnp.float32, jnp.bfloat16
MESH = pl.DeviceIdType.MESH
FIRST = (0, 1, 3, 6)


def remote(src, dst, send_sem, recv_sem, device):
    return pltpu.make_async_remote_copy(
        src_ref=src,
        dst_ref=dst,
        send_sem=send_sem,
        recv_sem=recv_sem,
        device_id=device,
        device_id_type=MESH,
    )


def arrived(ref, sem):
    pltpu.make_async_copy(ref, ref, sem).wait()


def split(value):
    high = value.astype(BF16)
    return high, (value - high.astype(F32)).astype(BF16)


def dot3(a, b, dims):
    def one(u, v):
        return lax.dot_general(u, v, (dims, ((), ())), preferred_element_type=F32)

    return one(a[0], b[0]) + (one(a[0], b[1]) + one(a[1], b[0]))


def kernel(
    t_ref, p_ref, i_ref, c_ref, u_out, c_out, e_out,
    inv, pr, pz, tt, tx, tr, lr, lz, ut, ux, ur, fin, fx,
    p_hi, p_lo, w_hi, w_lo, lr_hi, lr_lo, lc_hi, lc_lo,
    inv_s, inv_r, inv2_s, inv2_r, a_s, a_r, b_s, b_r, x_s, x_r, z_s, z_r, z2_s, z2_r,
    t_s, t_r, tr_s, tr_r, l_s, l_r, ur_s, ur_r,
):
    row, col = lax.axis_index("row"), lax.axis_index("col")
    z, k = col // 2, lax.rem(col, 2)
    x, y = row // 4, lax.rem(row, 4)
    q, w = z // 4, lax.rem(z, 4)
    p = lax.rem(y + w, 4)
    sibling = (row, 2 * z + 1 - k)
    half, other = pl.ds(pl.multiple_of(128 * k, 128), 128), pl.ds(pl.multiple_of(128 * (1 - k), 128), 128)

    def along(d):
        return (row, 2 * lax.rem(z + d + 16, 16) + k)

    barrier = pltpu.get_barrier_semaphore()

    @pl.loop(1, 32)
    def _(d):
        pl.semaphore_signal(barrier, inc=1, device_id=(row, lax.rem(col + d, 32)), device_id_type=MESH)

    @pl.loop(1, 16)
    def _(d):
        pl.semaphore_signal(barrier, inc=1, device_id=(lax.rem(row + d, 16), col), device_id_type=MESH)

    @pl.when(row != z)
    def _():
        pl.semaphore_signal(barrier, inc=1, device_id=(z, 2 * row + k), device_id_type=MESH)

    pl.semaphore_wait(barrier, jnp.where(row != z, 47, 46))

    def to_transposed():
        return remote(p_ref, pz.at[k, z], z_s, z_r, (z, 2 * row + k))

    @pl.when(row != z)
    def _():
        to_transposed().start()

    @pl.when(row == z)
    def _():
        pltpu.make_async_copy(p_ref, pz.at[k, z], z_r).start()

    def stride4(d):
        return remote(p_ref, pr.at[w, k, q], a_s.at[d], a_r, along(4 * d))

    for d in (2, 1, 3):
        stride4(d).start()
    pltpu.make_async_copy(p_ref, pr.at[w, k, q], a_r).start()

    tile_rows = pl.ds(pl.multiple_of(8 * x, 8), 8)
    slot = p * (p + 1) // 2 + q

    def piece(d):
        to = lax.rem(col + d, 32)
        columns = pl.ds(pl.multiple_of(128 * (2 * p + lax.rem(to, 2)), 128), 128)
        return i_ref.at[tile_rows, columns], to

    def send_piece(d):
        src, to = piece(d)
        return remote(src, inv.at[row, slot, k], inv_s.at[d], inv_r, (row, to))

    @pl.when(p >= q)
    def _():
        @pl.loop(1, 32)
        def _(d):
            send_piece(d).start()

        src, _ = piece(0)
        pltpu.make_async_copy(src, inv.at[row, slot, k], inv_r).start()

    tt[...] = t_ref[...].T

    def share(buf, into, i):
        return remote(buf.at[:, other], into, t_s.at[i], t_r.at[i], sibling)

    share(tt, tx, 0).start()

    arrived(pz.at[k, row], z_r)

    def panel_plane(d):
        return remote(pz.at[k, row], pz.at[k, row], z2_s.at[d], z2_r, (lax.rem(row + d, 16), col))

    @pl.loop(1, 16)
    def _(d):
        panel_plane(d).start()

    arrived(pr.at[w, k], a_r)
    first_two, last_two = pr.at[w, k, pl.ds(0, 2)], pr.at[w, k, pl.ds(2, 2)]
    group = [
        remote(pr.at[w, k], pr.at[w, k], b_s.at[0], b_r.at[0], along(1)),
        remote(pr.at[w, k], pr.at[w, k], b_s.at[1], b_r.at[1], along(-1)),
        remote(first_two, first_two, b_s.at[2], b_r.at[2], along(2)),
        remote(last_two, last_two, b_s.at[3], b_r.at[3], along(-2)),
    ]
    for g in group:
        g.start()

    def swap(i, v):
        return remote(pr.at[v, k], pr.at[v, k], x_s.at[i], x_r.at[i], sibling)

    swap(0, w).start()

    arrived(inv.at[row], inv_r)

    def inv_plane(d):
        return remote(inv.at[row], inv.at[row], inv2_s.at[d], inv2_r, (lax.rem(row + d, 16), col))

    @pl.loop(1, 16)
    def _(d):
        inv_plane(d).start()

    def send_sums(buf, into, send_sem, recv_sem):
        def make(d):
            to = lax.rem(z + d, 16)
            return remote(buf.at[pl.ds(pl.multiple_of(8 * to, 8), 8), half], into.at[z], send_sem.at[d], recv_sem, (row, 2 * to + k))

        return make

    def start_sums(buf, other_half, into, i, send_sem, recv_sem):
        share(buf, other_half, i).wait()
        buf[:, half] += other_half[...]
        make = send_sums(buf, into, send_sem, recv_sem)

        @pl.loop(1, 16)
        def _(d):
            make(d).start()

        into[z] = buf[pl.ds(pl.multiple_of(8 * z, 8), 8), half]

    start_sums(tt, tx, tr, 0, tr_s, tr_r)

    left, right, far = lax.rem(w + 3, 4), lax.rem(w + 1, 4), lax.rem(w + 2, 4)
    arrived(pr.at[left, k], b_r.at[0])
    swap(1, left).start()
    arrived(pr.at[right, k], b_r.at[1])
    swap(2, right).start()
    arrived(first_two, b_r.at[2])
    arrived(last_two, b_r.at[3])
    swap(3, far).start()

    arrived(pz.at[k, pl.ds(0, 15)], z2_r)
    swap_z = remote(pz.at[k], pz.at[k], x_s.at[4], x_r.at[4], sibling)
    swap_z.start()

    for i, v in enumerate((w, left, right, far)):
        arrived(pr.at[v, 1 - k], x_r.at[i])
    for i, v in enumerate((w, left, right, far)):
        swap(i, v).wait_send()
    for v in range(4):
        for h in range(2):
            for g in range(4):
                at = 32 * (2 * (4 * g + v) + h)
                high, low = split(pr[v, h, g])
                p_hi[at : at + 32, 0:256] = high
                p_lo[at : at + 32, 0:256] = low
    arrived(pz.at[1 - k], x_r.at[4])
    for h in range(2):
        for g in range(16):
            at = 32 * (2 * g + h)
            high, low = split(pz[h, g])
            p_hi[at : at + 32, 256:512] = high
            p_lo[at : at + 32, 256:512] = low

    arrived(inv.at[pl.ds(0, 15)], inv2_r)

    def give(n):
        return (
            remote(lr.at[n], lr.at[n], l_s.at[0, n // 2], l_r.at[0, n // 2], sibling),
            remote(lz.at[n, other], lz.at[n, other], l_s.at[1, n // 2], l_r.at[1, n // 2], sibling),
        )

    for b in range(4):
        depth = 256 * (b + 1)
        for g in range(b + 1):
            for v in range(4):
                source_y = (b - v) % 4
                for h in range(2):
                    at = 64 * (4 * g + v) + 32 * h
                    for pair in range(2):
                        both = jnp.concatenate(
                            [inv[4 * (2 * pair + e) + source_y, FIRST[b] + g, h] for e in range(2)], axis=0
                        )
                        high, low = split(both)
                        w_hi[b, at + 16 * pair : at + 16 * pair + 16, :] = high
                        w_lo[b, at + 16 * pair : at + 16 * pair + 16, :] = low
        block = dot3(
            (p_hi[0:depth, :], p_lo[0:depth, :]),
            (w_hi[b, 0:depth, :], w_lo[b, 0:depth, :]),
            ((0,), (0,)),
        )
        n = 2 * b + k
        lr[n] = block[0:256]
        lz[n] = block[256:512]
        for g in give(n):
            g.start()

    for b in range(4):
        n = 2 * b + 1 - k
        arrived(lr.at[n], l_r.at[0, b])
        arrived(lz.at[n, half], l_r.at[1, b])
    for n in range(8):
        at = slice(128 * n, 128 * n + 128)
        lr_hi[:, at], lr_lo[:, at] = split(lr[n])
        lc_hi[:, at], lc_lo[:, at] = split(lz[n, half])
    product = dot3((lr_hi[...], lr_lo[...]), (lc_hi[...], lc_lo[...]), ((1,), (1,)))
    ut[...] = product.T
    share(ut, ux, 1).start()
    u_out[...] = t_ref[...] - product
    start_sums(ut, ux, ur, 1, ur_s, ur_r)
    arrived(tr.at[pl.ds(0, 15)], tr_r)
    fin[0] = jnp.sum(tr[...], axis=0)
    arrived(ur.at[pl.ds(0, 15)], ur_r)
    fin[1] = jnp.sum(ur[...], axis=0)
    last = remote(fin, fx, t_s.at[2], t_r.at[2], sibling)
    last.start()
    last.wait()
    even = k == 0
    mine, theirs = fin[...], fx[...]
    sums = jnp.concatenate([jnp.where(even, mine, theirs), jnp.where(even, theirs, mine)], axis=2)
    sums = jnp.where(even, sums[:, 0:4], sums[:, 4:8])
    c_out[...] = c_ref[...] - sums[1]
    e_out[...] = sums[0] - sums[1]

    @pl.when(row != z)
    def _():
        to_transposed().wait_send()

    for d in (1, 2, 3):
        stride4(d).wait_send()

    @pl.when(p >= q)
    def _():
        @pl.loop(1, 32)
        def _(d):
            send_piece(d).wait_send()

    for g in group:
        g.wait_send()
    swap_z.wait_send()
    for b in range(4):
        for g in give(2 * b + k):
            g.wait_send()

    @pl.loop(1, 16)
    def _(d):
        panel_plane(d).wait_send()
        inv_plane(d).wait_send()
        send_sums(tt, tr, tr_s, tr_r)(d).wait_send()
        send_sums(ut, ur, ur_s, ur_r)(d).wait_send()


def on_device(trailing, panel_block, inverse, checksum):
    vmem = pl.BlockSpec(memory_space=pltpu.VMEM)
    dma = pltpu.SemaphoreType.DMA
    updated, checksum_new, reencoded = pl.pallas_call(
        kernel,
        out_shape=(
            jax.ShapeDtypeStruct((256, 128), F32),
            jax.ShapeDtypeStruct((4, 256), F32),
            jax.ShapeDtypeStruct((4, 256), F32),
        ),
        in_specs=[vmem] * 4,
        out_specs=(vmem,) * 3,
        scratch_shapes=[
            pltpu.VMEM((16, 10, 2, 8, 128), F32),
            pltpu.VMEM((4, 2, 4, 32, 256), F32),
            pltpu.VMEM((2, 16, 32, 256), F32),
            pltpu.VMEM((128, 256), F32),
            pltpu.VMEM((128, 128), F32),
            pltpu.VMEM((16, 8, 128), F32),
            pltpu.VMEM((8, 256, 128), F32),
            pltpu.VMEM((8, 256, 128), F32),
            pltpu.VMEM((128, 256), F32),
            pltpu.VMEM((128, 128), F32),
            pltpu.VMEM((16, 8, 128), F32),
            pltpu.VMEM((2, 8, 128), F32),
            pltpu.VMEM((2, 8, 128), F32),
            pltpu.VMEM((1024, 512), BF16),
            pltpu.VMEM((1024, 512), BF16),
            pltpu.VMEM((4, 1024, 128), BF16),
            pltpu.VMEM((4, 1024, 128), BF16),
            pltpu.VMEM((256, 1024), BF16),
            pltpu.VMEM((256, 1024), BF16),
            pltpu.VMEM((128, 1024), BF16),
            pltpu.VMEM((128, 1024), BF16),
            dma((32,)), dma, dma((16,)), dma,
            dma((4,)), dma, dma((4,)), dma((4,)),
            dma((5,)), dma((5,)), dma, dma, dma((16,)), dma,
            dma((3,)), dma((3,)), dma((16,)), dma,
            dma((2, 4)), dma((2, 4)), dma((16,)), dma,
        ],
        compiler_params=pltpu.CompilerParams(
            collective_id=0, has_side_effects=True, vmem_limit_bytes=32 * 1024 * 1024
        ),
    )(trailing, panel_block.T, inverse.T, checksum.T)
    return updated, checksum_new.T, reencoded.T


def solution(mesh):
    in_specs = (P("row", "col"), P("row", "col"), P(None, "col"), P("row", "col"))
    out_specs = (P("row", "col"), P("row", "col"), P("row", "col"))
    return jax.shard_map(
        on_device, mesh=mesh, in_specs=in_specs, out_specs=out_specs, check_vma=False
    )
```

time: 498 us -> 83.1 us (0.17)
  the two profiles are of different devices: /device:TPU:1 before, /device:TPU:29 now
where the time goes in v1:
time: 83.1 us; the launch traced here: 82.9 us
  Pallas kernels  77.1 us (93%)
  local copies, waits for them, and re-layouts  5.09 us (6%)
    pallas_call x1, Pallas kernels, on_device(): pl.pallas_call(kernel, out_shape=(jax.ShapeDtypeStruct((256, 128), F32),...  77.1 us
    unnamed x11, local copies, waits for them, and re-layouts  5.09 us

profile of v1, /device:TPU:29, one launch (start us, length us, event | category | flops | bytes accessed | tf_op | source)
XLA Modules:
  0.0 82.9 jit_solution(15334524838693658249)
XLA Ops:
  0.6 0.0 copy-start.3
  0.6 0.7 copy-done.3
  1.3 0.0 copy-start
  1.3 0.9 %copy-done = f32[256,128]{1,0:T(8,128)S(1)} copy-done((f32[256,128]{1,0:T(8,128)S(1)}, f32[256,128]{1,0:T(8,128)}, u32[]{:S(2)}) %copy-start) | copy-done | bytes 131096
  2.2 0.0 copy-start.1
  2.2 0.9 %copy-done.1 = f32[1024,32]{0,1:T(8,128)S(1)} copy-done((f32[1024,32]{0,1:T(8,128)S(1)}, f32[1024,32]{0,1:T(8,128)}, u32[]{:S(2)}) %copy-start.1) | copy-done | bytes 131096
  3.1 0.0 copy-start.2
  3.1 0.8 copy-done.2
  3.9 77.1 %shard_map.67 = (f32[256,128]{1,0:T(8,128)S(1)}, f32[4,256]{1,0:T(4,128)S(1)}, f32[4,256]{1,0:T(4,128)S(1)}) custom-call(f32[256,128]{1,0:T(8,128)S(1)} %copy-done, f32[32,256]{1,0:T(8,128)S(1)} %bitcast.6, f32[32,1024]{1,0:T(8,128)S(1)} %bitcast.5, f32[4,256]{1,0:T(4,128)S(1)} %bitcast.7), custom_call_target="tpu_custom_call" | custom-call | tf_op jit(solution)/shard_map/pallas_call | solution.py:297
  81.0 0.7 copy.10
  81.7 0.6 copy.11
  82.3 0.6 copy.12
Async XLA Ops:
  0.6 0.7 copy-start.3
  1.3 0.9 %copy-start = (f32[256,128]{1,0:T(8,128)S(1)}, f32[256,128]{1,0:T(8,128)}, u32[]{:S(2)}) copy-start(f32[256,128]{1,0:T(8,128)} %t_ref.1) | copy-start | bytes 393220
  2.2 0.9 %copy-start.1 = (f32[1024,32]{0,1:T(8,128)S(1)}, f32[1024,32]{0,1:T(8,128)}, u32[]{:S(2)}) copy-start(f32[1024,32]{0,1:T(8,128)} %param.6) | copy-start | bytes 393220
  3.1 0.8 copy-start.2

commit v2 on v1

v2 whole, which is shorter than its diff:
```python
import jax
import jax.numpy as jnp
from jax import lax
from jax.experimental import pallas as pl
from jax.experimental.pallas import tpu as pltpu
from jax.sharding import PartitionSpec as P

F32, BF16 = jnp.float32, jnp.bfloat16
MESH = pl.DeviceIdType.MESH
FIRST = (0, 1, 3, 6)


def remote(src, dst, send_sem, recv_sem, device):
    return pltpu.make_async_remote_copy(
        src_ref=src,
        dst_ref=dst,
        send_sem=send_sem,
        recv_sem=recv_sem,
        device_id=device,
        device_id_type=MESH,
    )


def arrived(ref, sem):
    pltpu.make_async_copy(ref, ref, sem).wait()


def split(value):
    high = value.astype(BF16)
    return high, (value - high.astype(F32)).astype(BF16)


def dot3(a, b, dims):
    def one(u, v):
        return lax.dot_general(u, v, (dims, ((), ())), preferred_element_type=F32)

    return one(a[0], b[0]) + (one(a[0], b[1]) + one(a[1], b[0]))


def kernel(
    t_ref, p_ref, i_ref, c_ref, u_out, c_out, e_out,
    tv, pv, iv, cv, inv, pr, pz, p2, ps1, ps2, ps, tt, tx, tr, fin, fx, gb, rb,
    p_hi, p_lo, w_hi, w_lo, lr_hi, lr_lo, lc_hi, lc_lo,
    in_s, inv_s, inv_r, near_s, near_r, far_s, far_r, a_s, a_r, b_s, b_r, x_s, x_r,
    z_s, z_r, z2_s, z2_r, p1_s, p1_r, p3_s, p3_r, p4_s, p4_r, t_s, t_r, tr_s, tr_r, l_s, l_r,
):
    loads = [
        pltpu.make_async_copy(i_ref, iv, in_s.at[0]),
        pltpu.make_async_copy(p_ref, pv, in_s.at[1]),
        pltpu.make_async_copy(t_ref, tv, in_s.at[2]),
        pltpu.make_async_copy(c_ref, cv, in_s.at[3]),
    ]
    for load in loads:
        load.start()
    row, col = lax.axis_index("row"), lax.axis_index("col")
    z, k = col // 2, lax.rem(col, 2)
    x, y = row // 4, lax.rem(row, 4)
    q, w = z // 4, lax.rem(z, 4)
    p = lax.rem(y + w, 4)
    even = k == 0
    sibling = (row, 2 * z + 1 - k)
    half, other = pl.ds(pl.multiple_of(128 * k, 128), 128), pl.ds(pl.multiple_of(128 * (1 - k), 128), 128)

    def along(d):
        return (row, 2 * lax.rem(z + d + 16, 16) + k)

    barrier = pltpu.get_barrier_semaphore()

    @pl.loop(1, 32)
    def _(d):
        pl.semaphore_signal(barrier, inc=1, device_id=(row, lax.rem(col + d, 32)), device_id_type=MESH)

    @pl.loop(1, 16)
    def _(d):
        pl.semaphore_signal(barrier, inc=1, device_id=(lax.rem(row + d, 16), col), device_id_type=MESH)

    @pl.when(row != z)
    def _():
        pl.semaphore_signal(barrier, inc=1, device_id=(z, 2 * row + k), device_id_type=MESH)

    loads[1].wait()
    p2[...] = jnp.zeros_like(p2)
    p2[:, 0:32] = (pv[:, 0:128] + pv[:, 128:256]).T
    loads[2].wait()
    tt[...] = tv[...].T
    for b in range(2):
        nothing = jnp.zeros((256, 128), BF16)
        w_hi[b, 512 * b + 256 : 512 * b + 512, 0:128] = nothing
        w_lo[b, 512 * b + 256 : 512 * b + 512, 0:128] = nothing
    loads[0].wait()
    loads[3].wait()
    pl.semaphore_wait(barrier, jnp.where(row != z, 47, 46))

    tile_rows = pl.ds(pl.multiple_of(8 * x, 8), 8)
    slot = p * (p + 1) // 2 + q
    outer, inner = jnp.where(even, y, x), jnp.where(even, x, y)

    def piece(d):
        to = lax.rem(col + d, 32)
        columns = pl.ds(pl.multiple_of(128 * (2 * p + lax.rem(to, 2)), 128), 128)
        return iv.at[tile_rows, columns], to

    def send_piece(d):
        src, to = piece(d)
        return remote(src, inv.at[k, outer, inner, slot], inv_s.at[d], inv_r.at[k], (row, to))

    @pl.when(p >= q)
    def _():
        @pl.loop(1, 32)
        def _(d):
            send_piece(d).start()

        src, _ = piece(0)
        pltpu.make_async_copy(src, inv.at[k, outer, inner, slot], inv_r.at[k]).start()

    def to_transposed():
        return remote(pv, pz.at[k, z], z_s, z_r, (z, 2 * row + k))

    @pl.when(row != z)
    def _():
        to_transposed().start()

    @pl.when(row == z)
    def _():
        pltpu.make_async_copy(pv, pz.at[k, z], z_r).start()

    def stride4(d):
        return remote(pv, pr.at[w, k, q], a_s.at[d], a_r, along(4 * d))

    for d in (2, 1, 3):
        stride4(d).start()
    pltpu.make_async_copy(pv, pr.at[w, k, q], a_r).start()

    def panel_sum(d):
        to = lax.rem(row + d, 16)
        return remote(p2.at[pl.ds(pl.multiple_of(8 * to, 8), 8)], ps1.at[row], p1_s.at[d], p1_r, (to, col))

    @pl.loop(1, 16)
    def _(d):
        panel_sum(d).start()

    ps1[row] = p2[pl.ds(pl.multiple_of(8 * row, 8), 8)]

    share = remote(tt.at[:, other], tx, t_s.at[0], t_r.at[0], sibling)
    share.start()

    place = ((y, x), (x, y))

    def device(h, o, i):
        return (4 * i + o if h == 0 else 4 * o + i, col)

    def near(h, d):
        o, i = place[h]
        ref = inv.at[h, o, i]
        return remote(ref, ref, near_s.at[h, d - 1], near_r.at[h, d - 1], device(h, o, lax.rem(i + d, 4)))

    def far(h, back, d):
        o, i = place[h]
        ref = inv.at[h, o, lax.rem(i + 4 - back, 4)]
        return remote(ref, ref, far_s.at[h, back, d - 1], far_r.at[h], device(h, lax.rem(o + d, 4), i))

    for h in range(2):
        o, i = place[h]
        arrived(inv.at[h, o, i], inv_r.at[h])
        for d in (2, 1, 3):
            near(h, d).start()
        for d in (2, 1, 3):
            far(h, 0, d).start()

    arrived(pz.at[k, row], z_r)

    def panel_plane(d):
        return remote(pz.at[k, row], pz.at[k, row], z2_s.at[d], z2_r, (lax.rem(row + d, 16), col))

    @pl.loop(1, 16)
    def _(d):
        panel_plane(d).start()

    arrived(ps1.at[pl.ds(0, 15)], p1_r)
    ps2[...] = jnp.sum(ps1[...], axis=0)

    def sum_transposed():
        return remote(ps2, ps.at[k, z], p3_s, p3_r, (z, 2 * row + k))

    @pl.when(row != z)
    def _():
        sum_transposed().start()

    @pl.when(row == z)
    def _():
        pltpu.make_async_copy(ps2, ps.at[k, z], p3_r).start()

    arrived(pr.at[w, k], a_r)
    first_two, last_two = pr.at[w, k, pl.ds(0, 2)], pr.at[w, k, pl.ds(2, 2)]
    group = [
        remote(first_two, first_two, b_s.at[2], b_r.at[2], along(2)),
        remote(last_two, last_two, b_s.at[3], b_r.at[3], along(-2)),
        remote(pr.at[w, k], pr.at[w, k], b_s.at[0], b_r.at[0], along(1)),
        remote(pr.at[w, k], pr.at[w, k], b_s.at[1], b_r.at[1], along(-1)),
    ]
    for g in group:
        g.start()

    def swap(i, v):
        return remote(pr.at[v, k], pr.at[v, k], x_s.at[i], x_r.at[i], sibling)

    swap(0, w).start()

    for d in (1, 3, 2):
        for h in range(2):
            o, i = place[h]
            arrived(inv.at[h, o, lax.rem(i + 4 - d, 4)], near_r.at[h, d - 1])
            for e in (2, 1, 3):
                far(h, d, e).start()

    arrived(ps.at[k, row], p3_r)

    def sum_plane(d):
        return remote(ps.at[k, row], ps.at[k, row], p4_s.at[d], p4_r, (lax.rem(row + d, 16), col))

    @pl.loop(1, 16)
    def _(d):
        sum_plane(d).start()

    share.wait()
    tt[:, half] += tx[...]

    def block_sum(d):
        to = lax.rem(z + d, 16)
        return remote(tt.at[pl.ds(pl.multiple_of(8 * to, 8), 8), half], tr.at[z], tr_s.at[d], tr_r, (row, 2 * to + k))

    @pl.loop(1, 16)
    def _(d):
        block_sum(d).start()

    tr[z] = tt[pl.ds(pl.multiple_of(8 * z, 8), 8), half]

    left, right, across = lax.rem(w + 3, 4), lax.rem(w + 1, 4), lax.rem(w + 2, 4)
    arrived(pr.at[left, k], b_r.at[0])
    swap(1, left).start()
    arrived(pr.at[right, k], b_r.at[1])
    swap(2, right).start()
    arrived(first_two, b_r.at[2])
    arrived(last_two, b_r.at[3])
    swap(3, across).start()

    arrived(pz.at[k, pl.ds(0, 15)], z2_r)
    swap_z = remote(pz.at[k], pz.at[k], x_s.at[4], x_r.at[4], sibling)
    swap_z.start()
    arrived(ps.at[k, pl.ds(0, 15)], p4_r)
    swap_s = remote(ps.at[k], ps.at[k], x_s.at[5], x_r.at[5], sibling)
    swap_s.start()

    for i, v in enumerate((w, left, right, across)):
        arrived(pr.at[v, 1 - k], x_r.at[i])
    for i, v in enumerate((w, left, right, across)):
        swap(i, v).wait_send()
    for m in range(8):
        parts = [pr[2 * (m % 2) + e // 2, e % 2, m // 2] for e in range(4)]
        at = slice(128 * m, 128 * m + 128)
        p_hi[0:256, at], p_lo[0:256, at] = split(jnp.concatenate(parts, axis=0).T)
    arrived(pz.at[1 - k], x_r.at[4])
    for m in range(8):
        parts = [pz[e % 2, 2 * m + e // 2] for e in range(4)]
        at = slice(128 * m, 128 * m + 128)
        p_hi[256:512, at], p_lo[256:512, at] = split(jnp.concatenate(parts, axis=0).T)
    arrived(ps.at[1 - k], x_r.at[5])
    for m in range(8):
        parts = jnp.concatenate([ps[e % 2, 2 * m + e // 2][:, 0:32] for e in range(4)], axis=1)
        at = slice(128 * m, 128 * m + 128)
        p_hi[512:528, at], p_lo[512:528, at] = split(jnp.concatenate([parts, jnp.zeros_like(parts)], axis=0))

    arrived(tr.at[pl.ds(0, 15)], tr_r)
    fin[...] = jnp.sum(tr[...], axis=0)
    last = remote(fin, fx, t_s.at[1], t_r.at[1], sibling)
    last.start()

    for h in range(2):
        arrived(inv.at[h, pl.ds(0, 3)], far_r.at[h])

    def put(at, rows, c_rows, s_rows):
        lr_hi[:, at], lr_lo[:, at] = split(rows)
        high, low = split(jnp.concatenate([c_rows, s_rows, jnp.zeros_like(s_rows)], axis=0))
        lc_hi[:, at], lc_lo[:, at] = high, low

    def give(b):
        return remote(gb.at[b], rb.at[b], l_s.at[b], l_r.at[b], sibling)

    for b in range(2):
        depth = 512 * (b + 1)
        for e in range(2):
            n = 2 * b + e
            for g in range(n + 1):
                for v in range(4):
                    sy = (n - v) % 4
                    for h in range(2):
                        at = 64 * (4 * g + v) + 32 * h
                        tiles = [inv[h, sy, sx, FIRST[n] + g] if h == 0 else inv[h, sx, sy, FIRST[n] + g] for sx in range(4)]
                        high, low = split(jnp.concatenate(tiles, axis=0))
                        w_hi[b, at : at + 32, 128 * e : 128 * e + 128] = high
                        w_lo[b, at : at + 32, 128 * e : 128 * e + 128] = low
        block = dot3(
            (p_hi[:, 0:depth], p_lo[:, 0:depth]),
            (w_hi[b, 0:depth, :], w_lo[b, 0:depth, :]),
            ((1,), (0,)),
        )
        one, two = block[256:384], block[384:512]
        gb[b, 0:256] = block[0:256]
        gb[b, 256:384] = jnp.where(even, two, one)
        gb[b, 384:392] = block[512:520]
        give(b).start()
        put(slice(512 * b, 512 * b + 256), block[0:256], jnp.where(even, one, two), block[512:520])

    for b in range(2):
        arrived(rb.at[b], l_r.at[b])
        put(slice(512 * b + 256, 512 * b + 512), rb[b, 0:256], rb[b, 256:384], rb[b, 384:392])
    product = dot3((lr_hi[...], lr_lo[...]), (lc_hi[...], lc_lo[...]), ((1,), (1,)))
    u_out[...] = tv[...] - product[:, 0:128]
    correction = product[:, 128:136].T
    correction = jnp.where(even, correction[0:4], correction[4:8])
    last.wait()
    mine, theirs = fin[...], fx[...]
    sums = jnp.concatenate([jnp.where(even, mine, theirs), jnp.where(even, theirs, mine)], axis=1)
    c_out[...] = cv[...] - correction
    e_out[...] = jnp.where(even, sums[0:4], sums[4:8]) - correction

    @pl.when(row != z)
    def _():
        to_transposed().wait_send()
        sum_transposed().wait_send()

    for d in (1, 2, 3):
        stride4(d).wait_send()

    @pl.when(p >= q)
    def _():
        @pl.loop(1, 32)
        def _(d):
            send_piece(d).wait_send()

    for g in group:
        g.wait_send()
    swap_z.wait_send()
    swap_s.wait_send()
    for b in range(2):
        give(b).wait_send()
    for h in range(2):
        for d in (1, 2, 3):
            near(h, d).wait_send()
            for back in range(4):
                far(h, back, d).wait_send()

    @pl.loop(1, 16)
    def _(d):
        panel_plane(d).wait_send()
        panel_sum(d).wait_send()
        sum_plane(d).wait_send()
        block_sum(d).wait_send()


def on_device(trailing, panel_block, inverse, checksum):
    vmem = pl.BlockSpec(memory_space=pltpu.VMEM)
    dma = pltpu.SemaphoreType.DMA
    updated, checksum_new, reencoded = pl.pallas_call(
        kernel,
        out_shape=(
            jax.ShapeDtypeStruct((256, 128), F32),
            jax.ShapeDtypeStruct((4, 256), F32),
            jax.ShapeDtypeStruct((4, 256), F32),
        ),
        in_specs=[pl.BlockSpec(memory_space=pltpu.HBM)] * 4,
        out_specs=(vmem,) * 3,
        scratch_shapes=[
            pltpu.VMEM((256, 128), F32),
            pltpu.VMEM((32, 256), F32),
            pltpu.VMEM((32, 1024), F32),
            pltpu.VMEM((4, 256), F32),
            pltpu.VMEM((2, 4, 4, 10, 8, 128), F32),
            pltpu.VMEM((4, 2, 4, 32, 256), F32),
            pltpu.VMEM((2, 16, 32, 256), F32),
            pltpu.VMEM((128, 128), F32),
            pltpu.VMEM((16, 8, 128), F32),
            pltpu.VMEM((8, 128), F32),
            pltpu.VMEM((2, 16, 8, 128), F32),
            pltpu.VMEM((128, 256), F32),
            pltpu.VMEM((128, 128), F32),
            pltpu.VMEM((16, 8, 128), F32),
            pltpu.VMEM((8, 128), F32),
            pltpu.VMEM((8, 128), F32),
            pltpu.VMEM((2, 392, 256), F32),
            pltpu.VMEM((2, 392, 256), F32),
            pltpu.VMEM((528, 1024), BF16),
            pltpu.VMEM((528, 1024), BF16),
            pltpu.VMEM((2, 1024, 256), BF16),
            pltpu.VMEM((2, 1024, 256), BF16),
            pltpu.VMEM((256, 1024), BF16),
            pltpu.VMEM((256, 1024), BF16),
            pltpu.VMEM((144, 1024), BF16),
            pltpu.VMEM((144, 1024), BF16),
            dma((4,)), dma((32,)), dma((2,)), dma((2, 3)), dma((2, 3)), dma((2, 4, 3)), dma((2,)),
            dma((4,)), dma, dma((4,)), dma((4,)), dma((6,)), dma((6,)),
            dma, dma, dma((16,)), dma, dma((16,)), dma, dma, dma, dma((16,)), dma,
            dma((2,)), dma((2,)), dma((16,)), dma, dma((2,)), dma((2,)),
        ],
        compiler_params=pltpu.CompilerParams(
            collective_id=0, has_side_effects=True, vmem_limit_bytes=48 * 1024 * 1024
        ),
    )(trailing, panel_block.T, inverse.T, checksum.T)
    return updated, checksum_new.T, reencoded.T


def solution(mesh):
    in_specs = (P("row", "col"), P("row", "col"), P(None, "col"), P("row", "col"))
    out_specs = (P("row", "col"), P("row", "col"), P("row", "col"))
    return jax.shard_map(
        on_device, mesh=mesh, in_specs=in_specs, out_specs=out_specs, check_vma=False
    )
```

time: 83.1 us -> 67.1 us (0.81)
  the two profiles are of different devices: /device:TPU:29 before, /device:TPU:1 now
where the time goes in v2:
time: 67.1 us; the launch traced here: 66.9 us
  Pallas kernels  61.1 us (91%)
  local copies, waits for them, and re-layouts  5.09 us (8%)
    pallas_call x1, Pallas kernels, on_device(): pl.pallas_call(kernel, out_shape=(jax.ShapeDtypeStruct((256, 128), F32),...  61.1 us
    unnamed x11, local copies, waits for them, and re-layouts  5.09 us

profile of v2, /device:TPU:1, one launch (start us, length us, event | category | flops | bytes accessed | tf_op | source)
XLA Modules:
  0.0 66.9 jit_solution(7909248336087724564)
XLA Ops:
  0.6 0.0 copy-start.3
  0.6 0.7 %copy-done.3 = f32[256,4]{0,1:T(4,128)S(1)} copy-done((f32[256,4]{0,1:T(4,128)S(1)}, f32[256,4]{0,1:T(4,128)}, u32[]{:S(2)}) %copy-start.3) | copy-done | bytes 4120
  1.3 0.0 copy-start
  1.3 0.9 %copy-done = f32[256,128]{1,0:T(8,128)S(1)} copy-done((f32[256,128]{1,0:T(8,128)S(1)}, f32[256,128]{1,0:T(8,128)}, u32[]{:S(2)}) %copy-start) | copy-done | bytes 131096
  2.2 0.0 copy-start.1
  2.2 0.9 %copy-done.1 = f32[1024,32]{0,1:T(8,128)S(1)} copy-done((f32[1024,32]{0,1:T(8,128)S(1)}, f32[1024,32]{0,1:T(8,128)}, u32[]{:S(2)}) %copy-start.1) | copy-done | bytes 131096
  3.1 0.0 copy-start.2
  3.1 0.8 %copy-done.2 = f32[256,32]{0,1:T(8,128)S(1)} copy-done((f32[256,32]{0,1:T(8,128)S(1)}, f32[256,32]{0,1:T(8,128)}, u32[]{:S(2)}) %copy-start.2) | copy-done | bytes 32792
  3.9 61.1 %shard_map.67 = (f32[256,128]{1,0:T(8,128)S(1)}, f32[4,256]{1,0:T(4,128)S(1)}, f32[4,256]{1,0:T(4,128)S(1)}) custom-call(f32[256,128]{1,0:T(8,128)S(1)} %copy-done, f32[32,256]{1,0:T(8,128)S(1)} %bitcast.6, f32[32,1024]{1,0:T(8,128)S(1)} %bitcast.5, f32[4,256]{1,0:T(4,128)S(1)} %bitcast.7), custom_call_target="tpu_custom_call" | custom-call | tf_op jit(solution)/shard_map/pallas_call | solution.py:364
  65.0 0.7 copy.10
  65.7 0.6 copy.11
  66.3 0.6 copy.12
Async XLA Ops:
  0.6 0.7 %copy-start.3 = (f32[256,4]{0,1:T(4,128)S(1)}, f32[256,4]{0,1:T(4,128)}, u32[]{:S(2)}) copy-start(f32[256,4]{0,1:T(4,128)} %param.7) | copy-start | bytes 12292
  1.3 0.9 %copy-start = (f32[256,128]{1,0:T(8,128)S(1)}, f32[256,128]{1,0:T(8,128)}, u32[]{:S(2)}) copy-start(f32[256,128]{1,0:T(8,128)} %t_ref.1) | copy-start | bytes 393220
  2.2 0.9 %copy-start.1 = (f32[1024,32]{0,1:T(8,128)S(1)}, f32[1024,32]{0,1:T(8,128)}, u32[]{:S(2)}) copy-start(f32[1024,32]{0,1:T(8,128)} %param.6) | copy-start | bytes 393220
  3.1 0.8 %copy-start.2 = (f32[256,32]{0,1:T(8,128)S(1)}, f32[256,32]{0,1:T(8,128)}, u32[]{:S(2)}) copy-start(f32[256,32]{0,1:T(8,128)} %param.5) | copy-start | bytes 98308

commit v3 on v2

v3 whole, which is shorter than its diff:
```python
import jax
import jax.numpy as jnp
from jax import lax
from jax.experimental import pallas as pl
from jax.experimental.pallas import tpu as pltpu
from jax.sharding import PartitionSpec as P

F32, BF16 = jnp.float32, jnp.bfloat16
MESH = pl.DeviceIdType.MESH
FIRST = (0, 1, 3, 6)


def remote(src, dst, send_sem, recv_sem, device):
    return pltpu.make_async_remote_copy(
        src_ref=src,
        dst_ref=dst,
        send_sem=send_sem,
        recv_sem=recv_sem,
        device_id=device,
        device_id_type=MESH,
    )


def arrived(ref, sem):
    pltpu.make_async_copy(ref, ref, sem).wait()


def split(value):
    high = value.astype(BF16)
    return high, (value - high.astype(F32)).astype(BF16)


def dot3(a, b, dims):
    def one(u, v):
        return lax.dot_general(u, v, (dims, ((), ())), preferred_element_type=F32)

    return one(a[0], b[0]) + (one(a[0], b[1]) + one(a[1], b[0]))


def kernel(
    t_ref, p_ref, i_ref, c_ref, u_out, c_out, e_out,
    tv, pv, cv, inv, pr, pz, p2, ps1, ps2, ps, tt, tx, tq, ta, tb, tc, fin, fx, gb, rb,
    p_hi, p_lo, w_hi, w_lo, lr_hi, lr_lo, lc_hi, lc_lo,
    in_s, near_s, near_r, far_s, far_r, a_s, a_r, b_s, b_r, x_s, x_r,
    z_s, z_r, z2_s, z2_r, p1_s, p1_r, p3_s, p3_r, p4_s, p4_r, t_s, t_r, ta_s, ta_r, tc_s, tc_r, l_s, l_r,
):
    row, col = lax.axis_index("row"), lax.axis_index("col")
    z, k = col // 2, lax.rem(col, 2)
    x, y = row // 4, lax.rem(row, 4)
    q, w = z // 4, lax.rem(z, 4)
    p = lax.rem(y + w, 4)
    even = k == 0
    tile_rows = pl.ds(pl.multiple_of(8 * x, 8), 8)
    loads = [
        pltpu.make_async_copy(p_ref, pv.at[pl.ds(0, 32)], in_s.at[0]),
        pltpu.make_async_copy(i_ref.at[tile_rows, pl.ds(pl.multiple_of(256 * p, 256), 256)], pv.at[pl.ds(32, 8)], in_s.at[1]),
        pltpu.make_async_copy(t_ref, tv, in_s.at[2]),
        pltpu.make_async_copy(c_ref, cv, in_s.at[3]),
    ]
    for load in loads:
        load.start()
    sibling = (row, 2 * z + 1 - k)
    half, other = pl.ds(pl.multiple_of(128 * k, 128), 128), pl.ds(pl.multiple_of(128 * (1 - k), 128), 128)

    def along(d):
        return (row, 2 * lax.rem(z + d + 16, 16) + k)

    barrier = pltpu.get_barrier_semaphore()

    for d in (8, 4, -4, 2, -2, 1, -1):
        pl.semaphore_signal(barrier, inc=1, device_id=along(d), device_id_type=MESH)
    pl.semaphore_signal(barrier, inc=1, device_id=sibling, device_id_type=MESH)

    @pl.loop(1, 16)
    def _(d):
        pl.semaphore_signal(barrier, inc=1, device_id=(lax.rem(row + d, 16), col), device_id_type=MESH)

    @pl.when(row != z)
    def _():
        pl.semaphore_signal(barrier, inc=1, device_id=(z, 2 * row + k), device_id_type=MESH)

    loads[0].wait()
    p2[...] = jnp.zeros_like(p2)
    p2[:, 0:32] = (pv[0:32, 0:128] + pv[0:32, 128:256]).T
    loads[2].wait()
    tt[...] = tv[...].T
    for b in range(2):
        nothing = jnp.zeros((256, 128), BF16)
        w_hi[b, 512 * b + 256 : 512 * b + 512, 0:128] = nothing
        w_lo[b, 512 * b + 256 : 512 * b + 512, 0:128] = nothing
    loads[1].wait()
    loads[3].wait()
    pl.semaphore_wait(barrier, jnp.where(row != z, 24, 23))

    def stride4(d):
        return remote(pv, pr.at[w, k, q], a_s.at[d], a_r.at[d], along(4 * d))

    def to_group(back):
        at = lax.rem(q + 4 - back, 4)
        src, dst = pr.at[w, k, at] if back else pv, pr.at[w, k, at]
        low = at < 2
        return [
            remote(src, dst, b_s.at[back, 2], b_r.at[jnp.where(low, 2, 3)], along(jnp.where(low, 2, -2))),
            remote(src, dst, b_s.at[back, 0], b_r.at[0], along(1)),
            remote(src, dst, b_s.at[back, 1], b_r.at[1], along(-1)),
        ]

    for d in (2, 1, 3):
        stride4(d).start()
    for g in to_group(0):
        g.start()
    pltpu.make_async_copy(pv, pr.at[w, k, q], a_r.at[0]).start()

    def to_transposed():
        return remote(pv.at[pl.ds(0, 32)], pz.at[k, z], z_s, z_r, (z, 2 * row + k))

    @pl.when(row != z)
    def _():
        to_transposed().start()

    @pl.when(row == z)
    def _():
        pltpu.make_async_copy(pv.at[pl.ds(0, 32)], pz.at[k, z], z_r).start()

    def panel_sum(d):
        to = lax.rem(row + d, 16)
        return remote(p2.at[pl.ds(pl.multiple_of(8 * to, 8), 8)], ps1.at[row], p1_s.at[d], p1_r, (to, col))

    @pl.loop(1, 16)
    def _(d):
        panel_sum(d).start()

    ps1[row] = p2[pl.ds(pl.multiple_of(8 * row, 8), 8)]

    share = remote(tt.at[:, other], tx, t_s.at[0], t_r.at[0], sibling)
    share.start()

    arrived(ps1.at[pl.ds(0, 15)], p1_r)
    ps2[...] = jnp.sum(ps1[...], axis=0)

    def sum_transposed():
        return remote(ps2, ps.at[k, z], p3_s, p3_r, (z, 2 * row + k))

    @pl.when(row != z)
    def _():
        sum_transposed().start()

    @pl.when(row == z)
    def _():
        pltpu.make_async_copy(ps2, ps.at[k, z], p3_r).start()

    for d in (1, 3, 2):
        arrived(pr.at[w, k, lax.rem(q + 4 - d, 4)], a_r.at[d])
        for g in to_group(d):
            g.start()
    arrived(pr.at[w, k, q], a_r.at[0])
    first_two, last_two = pr.at[w, k, pl.ds(0, 2)], pr.at[w, k, pl.ds(2, 2)]

    def swap(i, v):
        return remote(pr.at[v, k], pr.at[v, k], x_s.at[i], x_r.at[i], sibling)

    swap(0, w).start()

    arrived(pz.at[k, row], z_r)

    def panel_plane(d):
        return remote(pz.at[k, row], pz.at[k, row], z2_s.at[d], z2_r, (lax.rem(row + d, 16), col))

    @pl.loop(1, 16)
    def _(d):
        panel_plane(d).start()

    share.wait()
    tt[:, half] += tx[...]

    for d in range(16):
        tq[d % 4, d // 4] = tt[8 * d : 8 * d + 8, half]
    left, right, across = lax.rem(w + 3, 4), lax.rem(w + 1, 4), lax.rem(w + 2, 4)
    gather_sums = [
        remote(tq.at[left], ta.at[0], ta_s.at[0], ta_r.at[0], along(-1)),
        remote(tq.at[right], ta.at[1], ta_s.at[1], ta_r.at[1], along(1)),
        remote(tq.at[across, pl.ds(0, 2)], ta.at[2, pl.ds(0, 2)], ta_s.at[2], ta_r.at[2], along(2)),
        remote(tq.at[across, pl.ds(2, 2)], ta.at[2, pl.ds(2, 2)], ta_s.at[3], ta_r.at[3], along(-2)),
    ]
    for g in gather_sums:
        g.start()

    arrived(pr.at[left, k], b_r.at[0])
    swap(1, left).start()
    arrived(pr.at[right, k], b_r.at[1])
    swap(2, right).start()
    arrived(first_two, b_r.at[2])
    arrived(last_two, b_r.at[3])
    swap(3, across).start()

    place = ((y, x), (x, y))
    parity = (k, 1 - k)

    def device(h, o, i):
        return (4 * i + o if h == 0 else 4 * o + i, col)

    def near(h, d):
        o, i = place[h]
        ref = inv.at[h, o, i]
        return remote(ref, ref, near_s.at[h, d - 1], near_r.at[h, d - 1], device(h, o, lax.rem(i + d, 4)))

    def far(h, back, d):
        o, i = place[h]
        ref = inv.at[h, o, lax.rem(i + 4 - back, 4)]
        return remote(ref, ref, far_s.at[h, back, d - 1], far_r.at[h], device(h, lax.rem(o + d, 4), i))

    def pack(h):
        o, i = place[h]
        for n in range(4):
            for g in range(n + 1):
                inv[h, o, i, FIRST[n] + g] = pr[lax.rem(n + 4 - y, 4), parity[h], g, 32:40, half]
        for d in (2, 1, 3):
            near(h, d).start()
        for d in (2, 1, 3):
            far(h, 0, d).start()

    pack(0)
    arrived(ps.at[k, row], p3_r)

    def sum_plane(d):
        return remote(ps.at[k, row], ps.at[k, row], p4_s.at[d], p4_r, (lax.rem(row + d, 16), col))

    @pl.loop(1, 16)
    def _(d):
        sum_plane(d).start()

    for i, v in enumerate((w, left, right, across)):
        arrived(pr.at[v, 1 - k], x_r.at[i])
    pack(1)

    def forward(h, d):
        o, i = place[h]
        arrived(inv.at[h, o, lax.rem(i + 4 - d, 4)], near_r.at[h, d - 1])
        for e in (2, 1, 3):
            far(h, d, e).start()

    for d in (1, 3, 2):
        forward(0, d)
    for d in (1, 3, 2):
        forward(1, d)

    for i, g in enumerate(gather_sums):
        arrived((ta.at[i] if i < 2 else ta.at[2, pl.ds(2 * i - 4, 2)]), ta_r.at[i])
    tb[...] = tq[w] + ta[0] + ta[1] + ta[2]

    def block_sum(d):
        return remote(tb.at[lax.rem(q + d, 4)], tc.at[q], tc_s.at[d], tc_r, along(4 * d))

    for d in (2, 1, 3):
        block_sum(d).start()
    tc[q] = tb[q]

    arrived(pz.at[k, pl.ds(0, 15)], z2_r)
    swap_z = remote(pz.at[k], pz.at[k], x_s.at[4], x_r.at[4], sibling)
    swap_z.start()
    arrived(ps.at[k, pl.ds(0, 15)], p4_r)
    swap_s = remote(ps.at[k], ps.at[k], x_s.at[5], x_r.at[5], sibling)
    swap_s.start()

    for i, v in enumerate((w, left, right, across)):
        swap(i, v).wait_send()
    for m in range(8):
        parts = [pr[2 * (m % 2) + e // 2, parity[e % 2], m // 2, 0:32] for e in range(4)]
        at = slice(128 * m, 128 * m + 128)
        p_hi[0:256, at], p_lo[0:256, at] = split(jnp.concatenate(parts, axis=0).T)
    arrived(pz.at[1 - k], x_r.at[4])
    for m in range(8):
        parts = [pz[parity[e % 2], 2 * m + e // 2] for e in range(4)]
        at = slice(128 * m, 128 * m + 128)
        p_hi[256:512, at], p_lo[256:512, at] = split(jnp.concatenate(parts, axis=0).T)
    arrived(ps.at[1 - k], x_r.at[5])
    for m in range(8):
        parts = jnp.concatenate([ps[parity[e % 2], 2 * m + e // 2][:, 0:32] for e in range(4)], axis=1)
        at = slice(128 * m, 128 * m + 128)
        p_hi[512:528, at], p_lo[512:528, at] = split(jnp.concatenate([parts, jnp.zeros_like(parts)], axis=0))

    arrived(tc.at[pl.ds(0, 3)], tc_r)
    fin[...] = jnp.sum(tc[...], axis=0)
    last = remote(fin, fx, t_s.at[1], t_r.at[1], sibling)
    last.start()

    for h in range(2):
        arrived(inv.at[h, pl.ds(0, 3)], far_r.at[h])

    def put(at, rows, c_rows, s_rows):
        lr_hi[:, at], lr_lo[:, at] = split(rows)
        high, low = split(jnp.concatenate([c_rows, s_rows, jnp.zeros_like(s_rows)], axis=0))
        lc_hi[:, at], lc_lo[:, at] = high, low

    def give(b):
        return remote(gb.at[b], rb.at[b], l_s.at[b], l_r.at[b], sibling)

    for b in range(2):
        depth = 512 * (b + 1)
        for e in range(2):
            n = 2 * b + e
            for g in range(n + 1):
                for v in range(4):
                    sy = (n - v) % 4
                    for h in range(2):
                        at = 64 * (4 * g + v) + 32 * h
                        tiles = [inv[h, sy, sx, FIRST[n] + g] if h == 0 else inv[h, sx, sy, FIRST[n] + g] for sx in range(4)]
                        high, low = split(jnp.concatenate(tiles, axis=0))
                        w_hi[b, at : at + 32, 128 * e : 128 * e + 128] = high
                        w_lo[b, at : at + 32, 128 * e : 128 * e + 128] = low
        block = dot3(
            (p_hi[:, 0:depth], p_lo[:, 0:depth]),
            (w_hi[b, 0:depth, :], w_lo[b, 0:depth, :]),
            ((1,), (0,)),
        )
        one, two = block[256:384], block[384:512]
        gb[b, 0:256] = block[0:256]
        gb[b, 256:384] = jnp.where(even, two, one)
        gb[b, 384:392] = block[512:520]
        give(b).start()
        put(slice(512 * b, 512 * b + 256), block[0:256], jnp.where(even, one, two), block[512:520])

    for b in range(2):
        arrived(rb.at[b], l_r.at[b])
        put(slice(512 * b + 256, 512 * b + 512), rb[b, 0:256], rb[b, 256:384], rb[b, 384:392])
    product = dot3((lr_hi[...], lr_lo[...]), (lc_hi[...], lc_lo[...]), ((1,), (1,)))
    u_out[...] = tv[...] - product[:, 0:128]
    correction = product[:, 128:136].T
    correction = jnp.where(even, correction[0:4], correction[4:8])
    last.wait()
    mine, theirs = fin[...], fx[...]
    sums = jnp.concatenate([jnp.where(even, mine, theirs), jnp.where(even, theirs, mine)], axis=1)
    c_out[...] = cv[...] - correction
    e_out[...] = jnp.where(even, sums[0:4], sums[4:8]) - correction

    @pl.when(row != z)
    def _():
        to_transposed().wait_send()
        sum_transposed().wait_send()

    for d in (1, 2, 3):
        stride4(d).wait_send()
        block_sum(d).wait_send()

    for g in gather_sums + [g for back in range(4) for g in to_group(back)]:
        g.wait_send()
    swap_z.wait_send()
    swap_s.wait_send()
    for b in range(2):
        give(b).wait_send()
    for h in range(2):
        for d in (1, 2, 3):
            near(h, d).wait_send()
            for back in range(4):
                far(h, back, d).wait_send()

    @pl.loop(1, 16)
    def _(d):
        panel_plane(d).wait_send()
        panel_sum(d).wait_send()
        sum_plane(d).wait_send()


def on_device(trailing, panel_block, inverse, checksum):
    vmem = pl.BlockSpec(memory_space=pltpu.VMEM)
    dma = pltpu.SemaphoreType.DMA
    updated, checksum_new, reencoded = pl.pallas_call(
        kernel,
        out_shape=(
            jax.ShapeDtypeStruct((256, 128), F32),
            jax.ShapeDtypeStruct((4, 256), F32),
            jax.ShapeDtypeStruct((4, 256), F32),
        ),
        in_specs=[pl.BlockSpec(memory_space=pltpu.HBM)] * 4,
        out_specs=(vmem,) * 3,
        scratch_shapes=[
            pltpu.VMEM((256, 128), F32),
            pltpu.VMEM((40, 256), F32),
            pltpu.VMEM((4, 256), F32),
            pltpu.VMEM((2, 4, 4, 10, 8, 128), F32),
            pltpu.VMEM((4, 2, 4, 40, 256), F32),
            pltpu.VMEM((2, 16, 32, 256), F32),
            pltpu.VMEM((128, 128), F32),
            pltpu.VMEM((16, 8, 128), F32),
            pltpu.VMEM((8, 128), F32),
            pltpu.VMEM((2, 16, 8, 128), F32),
            pltpu.VMEM((128, 256), F32),
            pltpu.VMEM((128, 128), F32),
            pltpu.VMEM((4, 4, 8, 128), F32),
            pltpu.VMEM((3, 4, 8, 128), F32),
            pltpu.VMEM((4, 8, 128), F32),
            pltpu.VMEM((4, 8, 128), F32),
            pltpu.VMEM((8, 128), F32),
            pltpu.VMEM((8, 128), F32),
            pltpu.VMEM((2, 392, 256), F32),
            pltpu.VMEM((2, 392, 256), F32),
            pltpu.VMEM((528, 1024), BF16),
            pltpu.VMEM((528, 1024), BF16),
            pltpu.VMEM((2, 1024, 256), BF16),
            pltpu.VMEM((2, 1024, 256), BF16),
            pltpu.VMEM((256, 1024), BF16),
            pltpu.VMEM((256, 1024), BF16),
            pltpu.VMEM((144, 1024), BF16),
            pltpu.VMEM((144, 1024), BF16),
            dma((4,)), dma((2, 3)), dma((2, 3)), dma((2, 4, 3)), dma((2,)),
            dma((4,)), dma((4,)), dma((4, 3)), dma((4,)), dma((6,)), dma((6,)),
            dma, dma, dma((16,)), dma, dma((16,)), dma, dma, dma, dma((16,)), dma,
            dma((2,)), dma((2,)), dma((4,)), dma((4,)), dma((4,)), dma, dma((2,)), dma((2,)),
        ],
        compiler_params=pltpu.CompilerParams(
            collective_id=0, has_side_effects=True, vmem_limit_bytes=62 * 1024 * 1024
        ),
    )(trailing, panel_block.T, inverse.T, checksum.T)
    return updated, checksum_new.T, reencoded.T


def solution(mesh):
    in_specs = (P("row", "col"), P("row", "col"), P(None, "col"), P("row", "col"))
    out_specs = (P("row", "col"), P("row", "col"), P("row", "col"))
    return jax.shard_map(
        on_device, mesh=mesh, in_specs=in_specs, out_specs=out_specs, check_vma=False
    )
```

time: 67.1 us -> 65.9 us (0.982)
  local copies, waits for them, and re-layouts: 5.09 us -> 2.84 us
  Pallas kernels: 61.1 us -> 62.2 us
    unnamed x11 -> x7, local copies, waits for them, and re-layouts: 5.09 us -> 2.84 us
    pallas_call x1, Pallas kernels: 61.1 us -> 62.2 us  [on_device(): pl.pallas_call(kernel, out_shape=(jax.ShapeDtypeStruct((256, 128), F32),...]
where the time goes in v3:
time: 65.9 us; the launch traced here: 65.7 us
  Pallas kernels  62.2 us (94%)
  local copies, waits for them, and re-layouts  2.84 us (4%)
    pallas_call x1, Pallas kernels, on_device(): pl.pallas_call(kernel, out_shape=(jax.ShapeDtypeStruct((256, 128), F32),...  62.2 us
    unnamed x7, local copies, waits for them, and re-layouts  2.84 us

profile of v3, /device:TPU:1, one launch (start us, length us, event | category | flops | bytes accessed | tf_op | source)
XLA Modules:
  0.0 65.7 jit_solution(5685229123646467027)
XLA Ops:
  0.6 62.2 %shard_map.67 = (f32[256,128]{1,0:T(8,128)}, f32[4,256]{1,0:T(4,128)}, f32[4,256]{1,0:T(4,128)}) custom-call(f32[256,128]{1,0:T(8,128)} %t_ref.1, f32[32,256]{1,0:T(8,128)} %bitcast.6, f32[32,1024]{1,0:T(8,128)} %bitcast.5, f32[4,256]{1,0:T(4,128)} %bitcast.7), custom_call_target="tpu_custom_call" | custom-call | tf_op jit(solution)/shard_map/pallas_call | solution.py:367
  62.9 0.0 copy-start.1
  62.9 1.6 %copy.10 = f32[256,128]{1,0:T(8,128)} copy(f32[256,128]{1,0:T(8,128)} %get-tuple-element.12) | data formatting | bytes 262144
  64.4 0.0 copy-done.1
  64.4 0.0 copy-start
  64.4 0.6 copy.11
  65.0 0.1 copy-done
  65.1 0.6 copy.12
Async XLA Ops:
  62.9 1.6 %copy-start.1 = (f32[4,256]{1,0:T(4,128)S(1)}, f32[4,256]{1,0:T(4,128)}, u32[]{:S(2)}) copy-start(f32[4,256]{1,0:T(4,128)} %get-tuple-element.7) | copy-start | bytes 12292
  64.4 0.7 %copy-start = (f32[4,256]{1,0:T(4,128)S(1)}, f32[4,256]{1,0:T(4,128)}, u32[]{:S(2)}) copy-start(f32[4,256]{1,0:T(4,128)} %get-tuple-element.8) | copy-start | bytes 12292

commit v4 on v3

--- a/solution.py
+++ b/solution.py
@@ -39,7 +39,7 @@
 
 def kernel(
     t_ref, p_ref, i_ref, c_ref, u_out, c_out, e_out,
-    tv, pv, cv, inv, pr, pz, p2, ps1, ps2, ps, tt, tx, tq, ta, tb, tc, fin, fx, gb, rb,
+    tv, pv, cv, inv, pr, pz, p2, ps1, ps2, ps, tt, tx, tq, ta, tb, tc, fin, fx, gb, rb, part_0,
     p_hi, p_lo, w_hi, w_lo, lr_hi, lr_lo, lc_hi, lc_lo,
     in_s, near_s, near_r, far_s, far_r, a_s, a_r, b_s, b_r, x_s, x_r,
     z_s, z_r, z2_s, z2_r, p1_s, p1_r, p3_s, p3_r, p4_s, p4_r, t_s, t_r, ta_s, ta_r, tc_s, tc_r, l_s, l_r,
@@ -85,12 +85,25 @@
     loads[2].wait()
     tt[...] = tv[...].T
     for b in range(2):
-        nothing = jnp.zeros((256, 128), BF16)
-        w_hi[b, 512 * b + 256 : 512 * b + 512, 0:128] = nothing
-        w_lo[b, 512 * b + 256 : 512 * b + 512, 0:128] = nothing
+        nothing = jnp.zeros((128, 128), BF16)
+        for h in range(2):
+            empty = slice(512 * h + 256 * b + 128, 512 * h + 256 * b + 256)
+            w_hi[b, empty, 0:128] = nothing
+            w_lo[b, empty, 0:128] = nothing
     loads[1].wait()
     loads[3].wait()
     pl.semaphore_wait(barrier, jnp.where(row != z, 24, 23))
+
+    def to_transposed():
+        return remote(pv.at[pl.ds(0, 32)], pz.at[k, z], z_s, z_r, (z, 2 * row + k))
+
+    @pl.when(row != z)
+    def _():
+        to_transposed().start()
+
+    @pl.when(row == z)
+    def _():
+        pltpu.make_async_copy(pv.at[pl.ds(0, 32)], pz.at[k, z], z_r).start()
 
     def stride4(d):
         return remote(pv, pr.at[w, k, q], a_s.at[d], a_r.at[d], along(4 * d))
@@ -111,17 +124,6 @@
         g.start()
     pltpu.make_async_copy(pv, pr.at[w, k, q], a_r.at[0]).start()
 
-    def to_transposed():
-        return remote(pv.at[pl.ds(0, 32)], pz.at[k, z], z_s, z_r, (z, 2 * row + k))
-
-    @pl.when(row != z)
-    def _():
-        to_transposed().start()
-
-    @pl.when(row == z)
-    def _():
-        pltpu.make_async_copy(pv.at[pl.ds(0, 32)], pz.at[k, z], z_r).start()
-
     def panel_sum(d):
         to = lax.rem(row + d, 16)
         return remote(p2.at[pl.ds(pl.multiple_of(8 * to, 8), 8)], ps1.at[row], p1_s.at[d], p1_r, (to, col))
@@ -134,6 +136,15 @@
 
     share = remote(tt.at[:, other], tx, t_s.at[0], t_r.at[0], sibling)
     share.start()
+
+    arrived(pz.at[k, row], z_r)
+
+    def panel_plane(d):
+        return remote(pz.at[k, row], pz.at[k, row], z2_s.at[d], z2_r, (lax.rem(row + d, 16), col))
+
+    @pl.loop(1, 16)
+    def _(d):
+        panel_plane(d).start()
 
     arrived(ps1.at[pl.ds(0, 15)], p1_r)
     ps2[...] = jnp.sum(ps1[...], axis=0)
@@ -160,15 +171,6 @@
         return remote(pr.at[v, k], pr.at[v, k], x_s.at[i], x_r.at[i], sibling)
 
     swap(0, w).start()
-
-    arrived(pz.at[k, row], z_r)
-
-    def panel_plane(d):
-        return remote(pz.at[k, row], pz.at[k, row], z2_s.at[d], z2_r, (lax.rem(row + d, 16), col))
-
-    @pl.loop(1, 16)
-    def _(d):
-        panel_plane(d).start()
 
     share.wait()
     tt[:, half] += tx[...]
@@ -265,17 +267,17 @@
     for i, v in enumerate((w, left, right, across)):
         swap(i, v).wait_send()
     for m in range(8):
-        parts = [pr[2 * (m % 2) + e // 2, parity[e % 2], m // 2, 0:32] for e in range(4)]
+        parts = [pr[v, parity[m // 4], m % 4, 0:32] for v in range(4)]
         at = slice(128 * m, 128 * m + 128)
         p_hi[0:256, at], p_lo[0:256, at] = split(jnp.concatenate(parts, axis=0).T)
     arrived(pz.at[1 - k], x_r.at[4])
     for m in range(8):
-        parts = [pz[parity[e % 2], 2 * m + e // 2] for e in range(4)]
+        parts = [pz[parity[m // 4], 4 * (m % 4) + v] for v in range(4)]
         at = slice(128 * m, 128 * m + 128)
         p_hi[256:512, at], p_lo[256:512, at] = split(jnp.concatenate(parts, axis=0).T)
     arrived(ps.at[1 - k], x_r.at[5])
     for m in range(8):
-        parts = jnp.concatenate([ps[parity[e % 2], 2 * m + e // 2][:, 0:32] for e in range(4)], axis=1)
+        parts = jnp.concatenate([ps[parity[m // 4], 4 * (m % 4) + v][:, 0:32] for v in range(4)], axis=1)
         at = slice(128 * m, 128 * m + 128)
         p_hi[512:528, at], p_lo[512:528, at] = split(jnp.concatenate([parts, jnp.zeros_like(parts)], axis=0))
 
@@ -284,9 +286,6 @@
     last = remote(fin, fx, t_s.at[1], t_r.at[1], sibling)
     last.start()
 
-    for h in range(2):
-        arrived(inv.at[h, pl.ds(0, 3)], far_r.at[h])
-
     def put(at, rows, c_rows, s_rows):
         lr_hi[:, at], lr_lo[:, at] = split(rows)
         high, low = split(jnp.concatenate([c_rows, s_rows, jnp.zeros_like(s_rows)], axis=0))
@@ -295,24 +294,27 @@
     def give(b):
         return remote(gb.at[b], rb.at[b], l_s.at[b], l_r.at[b], sibling)
 
-    for b in range(2):
-        depth = 512 * (b + 1)
-        for e in range(2):
-            n = 2 * b + e
-            for g in range(n + 1):
-                for v in range(4):
-                    sy = (n - v) % 4
-                    for h in range(2):
-                        at = 64 * (4 * g + v) + 32 * h
+    blocks = [None, None]
+    for h in range(2):
+        arrived(inv.at[h, pl.ds(0, 3)], far_r.at[h])
+        for b in range(2):
+            for e in range(2):
+                n = 2 * b + e
+                for g in range(n + 1):
+                    for v in range(4):
+                        sy, at = (n - v) % 4, 512 * h + 32 * (4 * g + v)
                         tiles = [inv[h, sy, sx, FIRST[n] + g] if h == 0 else inv[h, sx, sy, FIRST[n] + g] for sx in range(4)]
                         high, low = split(jnp.concatenate(tiles, axis=0))
                         w_hi[b, at : at + 32, 128 * e : 128 * e + 128] = high
                         w_lo[b, at : at + 32, 128 * e : 128 * e + 128] = low
-        block = dot3(
-            (p_hi[:, 0:depth], p_lo[:, 0:depth]),
-            (w_hi[b, 0:depth, :], w_lo[b, 0:depth, :]),
-            ((1,), (0,)),
-        )
+            deep = slice(512 * h, 512 * h + 256 * (b + 1))
+            part = dot3((p_hi[:, deep], p_lo[:, deep]), (w_hi[b, deep, :], w_lo[b, deep, :]), ((1,), (0,)))
+            if h == 0:
+                part_0[b] = part
+            else:
+                blocks[b] = part
+    for b in range(2):
+        block = part_0[b] + blocks[b]
         one, two = block[256:384], block[384:512]
         gb[b, 0:256] = block[0:256]
         gb[b, 256:384] = jnp.where(even, two, one)
@@ -394,6 +396,7 @@
             pltpu.VMEM((8, 128), F32),
             pltpu.VMEM((2, 392, 256), F32),
             pltpu.VMEM((2, 392, 256), F32),
+            pltpu.VMEM((2, 528, 256), F32),
             pltpu.VMEM((528, 1024), BF16),
             pltpu.VMEM((528, 1024), BF16),
             pltpu.VMEM((2, 1024, 256), BF16),

time: 65.9 us -> 62.3 us (0.945)
  Pallas kernels: 62.2 us -> 58.7 us
    pallas_call x1, Pallas kernels: 62.2 us -> 58.7 us  [on_device(): pl.pallas_call(kernel, out_shape=(jax.ShapeDtypeStruct((256, 128), F32),...]
where the time goes in v4:
time: 62.3 us; the launch traced here: 62.1 us
  Pallas kernels  58.7 us (94%)
  local copies, waits for them, and re-layouts  2.84 us (5%)
  between operations  0.65 us (1%)
    pallas_call x1, Pallas kernels, on_device(): pl.pallas_call(kernel, out_shape=(jax.ShapeDtypeStruct((256, 128), F32),...  58.7 us
    unnamed x7, local copies, waits for them, and re-layouts  2.84 us

profile of v4, /device:TPU:1, one launch (start us, length us, event | category | flops | bytes accessed | tf_op | source)
XLA Modules:
  0.0 62.1 jit_solution(10885119824246194386)
XLA Ops:
  0.6 58.7 %shard_map.67 = (f32[256,128]{1,0:T(8,128)}, f32[4,256]{1,0:T(4,128)}, f32[4,256]{1,0:T(4,128)}) custom-call(f32[256,128]{1,0:T(8,128)} %t_ref.1, f32[32,256]{1,0:T(8,128)} %bitcast.6, f32[32,1024]{1,0:T(8,128)} %bitcast.5, f32[4,256]{1,0:T(4,128)} %bitcast.7), custom_call_target="tpu_custom_call" | custom-call | tf_op jit(solution)/shard_map/pallas_call | solution.py:369
  59.3 0.0 copy-start.1
  59.3 1.6 %copy.10 = f32[256,128]{1,0:T(8,128)} copy(f32[256,128]{1,0:T(8,128)} %get-tuple-element.12) | data formatting | bytes 262144
  60.9 0.0 copy-done.1
  60.9 0.0 copy-start
  60.9 0.6 copy.11
  61.5 0.1 copy-done
  61.5 0.6 copy.12
Async XLA Ops:
  59.3 1.6 %copy-start.1 = (f32[4,256]{1,0:T(4,128)S(1)}, f32[4,256]{1,0:T(4,128)}, u32[]{:S(2)}) copy-start(f32[4,256]{1,0:T(4,128)} %get-tuple-element.7) | copy-start | bytes 12292
  60.9 0.7 %copy-start = (f32[4,256]{1,0:T(4,128)S(1)}, f32[4,256]{1,0:T(4,128)}, u32[]{:S(2)}) copy-start(f32[4,256]{1,0:T(4,128)} %get-tuple-element.8) | copy-start | bytes 12292

commit v5 on v4

--- a/solution.py
+++ b/solution.py
@@ -411,9 +411,9 @@
             dma((2,)), dma((2,)), dma((4,)), dma((4,)), dma((4,)), dma, dma((2,)), dma((2,)),
         ],
         compiler_params=pltpu.CompilerParams(
-            collective_id=0, has_side_effects=True, vmem_limit_bytes=62 * 1024 * 1024
+            collective_id=0, has_side_effects=True, vmem_limit_bytes=48 * 1024 * 1024
         ),
-    )(trailing, panel_block.T, inverse.T, checksum.T)
+    )(*(pltpu.with_memory_space_constraint(v, pltpu.HBM) for v in (trailing, panel_block.T, inverse.T, checksum.T)))
     return updated, checksum_new.T, reencoded.T
 
 

time: 62.3 us -> 60.6 us (0.973)
  local copies, waits for them, and re-layouts: 2.84 us -> 1.84 us
  Pallas kernels: 58.7 us -> 58 us
    unnamed x7 -> x3, local copies, waits for them, and re-layouts: 2.84 us -> 1.84 us
    pallas_call x1, Pallas kernels: 58.7 us -> 58 us  [on_device(): pl.pallas_call(kernel, out_shape=(jax.ShapeDtypeStruct((256, 128), F32),...]
where the time goes in v5:
time: 60.6 us; the launch traced here: 60.5 us
  Pallas kernels  58 us (96%)
  local copies, waits for them, and re-layouts  1.84 us (3%)
  between operations  0.64 us (1%)
    pallas_call x1, Pallas kernels, on_device(): pl.pallas_call(kernel, out_shape=(jax.ShapeDtypeStruct((256, 128), F32),...  58 us
    unnamed x3, local copies, waits for them, and re-layouts  1.84 us

profile of v5, /device:TPU:1, one launch (start us, length us, event | category | flops | bytes accessed | tf_op | source)
XLA Modules:
  0.0 60.5 jit_solution(15930855759094999309)
XLA Ops:
  0.6 58.0 %shard_map.67 = (f32[256,128]{1,0:T(8,128)S(1)}, f32[4,256]{1,0:T(4,128)S(1)}, f32[4,256]{1,0:T(4,128)S(1)}) custom-call(f32[256,128]{1,0:T(8,128)} %t_ref.1, f32[32,256]{1,0:T(8,128)} %bitcast.8, f32[32,1024]{1,0:T(8,128)} %bitcast.7, f32[4,256]{1,0:T(4,128)} %bitcast.9), custom_call_target="tpu_custom_call" | custom-call | tf_op jit(solution)/shard_map/pallas_call | solution.py:369
  58.6 0.7 %copy.10 = f32[256,128]{1,0:T(8,128)} copy(f32[256,128]{1,0:T(8,128)S(1)} %get-tuple-element.12) | data formatting | bytes 262144
  59.3 0.6 copy.11
  59.9 0.6 copy.12

commit v6 on v5

--- a/solution.py
+++ b/solution.py
@@ -294,7 +294,6 @@
     def give(b):
         return remote(gb.at[b], rb.at[b], l_s.at[b], l_r.at[b], sibling)
 
-    blocks = [None, None]
     for h in range(2):
         arrived(inv.at[h, pl.ds(0, 3)], far_r.at[h])
         for b in range(2):
@@ -312,15 +311,13 @@
             if h == 0:
                 part_0[b] = part
             else:
-                blocks[b] = part
-    for b in range(2):
-        block = part_0[b] + blocks[b]
-        one, two = block[256:384], block[384:512]
-        gb[b, 0:256] = block[0:256]
-        gb[b, 256:384] = jnp.where(even, two, one)
-        gb[b, 384:392] = block[512:520]
-        give(b).start()
-        put(slice(512 * b, 512 * b + 256), block[0:256], jnp.where(even, one, two), block[512:520])
+                block = part_0[b] + part
+                one, two = block[256:384], block[384:512]
+                gb[b, 0:256] = block[0:256]
+                gb[b, 256:384] = jnp.where(even, two, one)
+                gb[b, 384:392] = block[512:520]
+                give(b).start()
+                put(slice(512 * b, 512 * b + 256), block[0:256], jnp.where(even, one, two), block[512:520])
 
     for b in range(2):
         arrived(rb.at[b], l_r.at[b])

time: 60.6 us -> 60.9 us (level)
  no operation moved by 1% of the time
where the time goes in v6:
time: 60.9 us; the launch traced here: 60.7 us
  Pallas kernels  58.2 us (96%)
  local copies, waits for them, and re-layouts  1.84 us (3%)
  between operations  0.64 us (1%)
    pallas_call x1, Pallas kernels, on_device(): pl.pallas_call(kernel, out_shape=(jax.ShapeDtypeStruct((256, 128), F32),...  58.2 us
    unnamed x3, local copies, waits for them, and re-layouts  1.84 us

profile of v6, /device:TPU:1, one launch (start us, length us, event | category | flops | bytes accessed | tf_op | source)
XLA Modules:
  0.0 60.7 jit_solution(12808507053244245156)
XLA Ops:
  0.6 58.2 %shard_map.67 = (f32[256,128]{1,0:T(8,128)S(1)}, f32[4,256]{1,0:T(4,128)S(1)}, f32[4,256]{1,0:T(4,128)S(1)}) custom-call(f32[256,128]{1,0:T(8,128)} %t_ref.1, f32[32,256]{1,0:T(8,128)} %bitcast.8, f32[32,1024]{1,0:T(8,128)} %bitcast.7, f32[4,256]{1,0:T(4,128)} %bitcast.9), custom_call_target="tpu_custom_call" | custom-call | tf_op jit(solution)/shard_map/pallas_call | solution.py:366
  58.9 0.7 %copy.10 = f32[256,128]{1,0:T(8,128)} copy(f32[256,128]{1,0:T(8,128)S(1)} %get-tuple-element.12) | data formatting | bytes 262144
  59.5 0.6 copy.11
  60.1 0.6 copy.12
